TPU v7x, 256 devices: a whole 4x4x8 slice. The times are simulated.
256 devices in a mesh: gx: 4 (over y), gy: 8 (over z), gz: 8 (over x, core).
Axes of the slice: x: 4, y: 4, z: 8, core: 2. Of those that a mesh axis runs over, the one named last changes fastest.
Arguments:
- right_side: float32 [16, 32, 64, 1024], P(None, 'gx', 'gy', 'gz'), may hold values from -21 to 21, as said below
- absorption: float32 [32, 64, 1024], P('gx', 'gy', 'gz'), may hold values from 0.25 to 4
- velocity: float32 [3, 32, 64, 1024], P(None, 'gx', 'gy', 'gz'), may hold values from -1 to 1
Outputs:
- solution_field: float32 [16, 32, 64, 1024], P(None, 'gx', 'gy', 'gz')
- residual: float32 [16, 32, 64, 1024], P(None, 'gx', 'gy', 'gz')
Inputs may be any that keep to these rules, and one draw needn't show every extreme that they name: `right_side`: Right-hand sides of order one, scaled from cell to cell.
All inputs are finite; a program needn't handle non-finite values.
Results may differ from a plain program's by a relative error of at most 0.0003.
Values sent between devices are 32-bit elements; how exact they have to be, the bound alone decides.
No kernel may reach another device: no remote copies, remote signals or barrier semaphores. Data moves between devices by JAX's collectives and lax.ppermute only.
A program may use at most 128 MiB of HBM per device.

v0:
```python
import jax
import jax.numpy as jnp
from jax import lax
from jax.sharding import PartitionSpec as P

STEPS = 4


def extended(cells, sides, width):
    for axis, dim in sides:
        count = lax.axis_size(axis)
        ends = count - 1
        head = lax.slice_in_dim(cells, 0, width, axis=dim)
        tail = lax.slice_in_dim(cells, cells.shape[dim] - width, cells.shape[dim], axis=dim)
        cells = jnp.concatenate(
            [
                lax.ppermute(tail, axis, [(i, (i + 1) % count) for i in range(ends)]),
                cells,
                lax.ppermute(head, axis, [((i + 1) % count, i) for i in range(ends)]),
            ],
            axis=dim,
        )
    return cells


def shifted_stencil(padded, coeff):
    center = padded[:, 1:-1, 1:-1, 1:-1]
    xplus = padded[:, 2:, 1:-1, 1:-1]
    xminus = padded[:, :-2, 1:-1, 1:-1]
    yplus = padded[:, 1:-1, 2:, 1:-1]
    yminus = padded[:, 1:-1, :-2, 1:-1]
    zplus = padded[:, 1:-1, 1:-1, 2:]
    zminus = padded[:, 1:-1, 1:-1, :-2]
    result = (6.0 + coeff[0]) * center - (xplus + xminus + yplus + yminus + zplus + zminus)
    result = result + 0.5 * (
        coeff[1] * (xplus - xminus) + coeff[2] * (yplus - yminus) + coeff[3] * (zplus - zminus)
    )
    return (result - 7.0 * center) / 6.0


def cholesky_solve(normal, target):
    lower = jnp.linalg.cholesky(normal)
    middle = lax.linalg.triangular_solve(lower, target, left_side=True, lower=True)
    return lax.linalg.triangular_solve(lower, middle, left_side=True, lower=True, transpose_a=True)


def small_solve(gram, count, steps):
    cols = count * (steps + 1)
    change = 7.0 * jnp.eye(cols, count * steps, dtype=gram.dtype) + 6.0 * jnp.eye(
        cols, count * steps, k=-count, dtype=gram.dtype
    )
    high = lax.Precision.HIGHEST
    gram_change = jnp.dot(gram, change, precision=high)
    normal = jnp.dot(change.T, gram_change, precision=high)
    target = jnp.dot(change.T, gram[:, :count], precision=high)
    coef = cholesky_solve(normal, target)
    return (coef, jnp.dot(change, coef, precision=high))


def shards(right_side, absorption, velocity):
    count, cells_x, cells_y, cells_z = right_side.shape
    coeff = jnp.concatenate([absorption[None], velocity], axis=0)
    blocks = [right_side]
    current = right_side
    for step in range(STEPS):
        padded = extended(current, (("gx", 1), ("gy", 2), ("gz", 3)), 1)
        current = shifted_stencil(padded, coeff)
        blocks.append(current)
    basis = jnp.stack(blocks).reshape(count * (STEPS + 1), -1)
    high = lax.Precision.HIGHEST
    local_gram = jnp.dot(basis, basis.T, precision=high)
    gram = lax.psum(local_gram, ("gx", "gy", "gz"))
    coef, mixed = small_solve(gram, count, STEPS)
    solution_field = jnp.dot(coef.T, basis[: count * STEPS], precision=high)
    residual = basis[:count] - jnp.dot(mixed.T, basis, precision=high)
    return (solution_field.reshape(right_side.shape), residual.reshape(right_side.shape))


def solution(mesh):
    return jax.shard_map(
        shards,
        mesh=mesh,
        in_specs=(P(None, "gx", "gy", "gz"), P("gx", "gy", "gz"), P(None, "gx", "gy", "gz")),
        out_specs=(P(None, "gx", "gy", "gz"), P(None, "gx", "gy", "gz")),
        check_vma=False,
    )
```

profile of v0, /device:TPU:2, one launch (start us, length us, event | category | flops | bytes accessed | tf_op | source)
XLA Modules:
  0.0 260.9 jit_solution(2480587713350939930)
XLA Ops:
  1.6 3.5 %collective-permute-start.1 = (f32[16,1,8,128]{3,2,1,0:T(8,128)S(1)}, f32[16,1,8,128]{3,2,1,0:T(8,128)S(1)}, u32[]{:S(2)}, u32[]{:S(2)}) collective-permute-start(f32[16,1,8,128]{3,2,1,0:T(8,128)S(1)} %get-tuple-element.51), channel_id=1, source_target_pairs={{0,64},{64,128},{128,192},{1,65},{65,129},{129,193},{2,66},{66,130... | collective-permute-start | bytes 196616 | tf_op jit(solution)/shard_map/ppermute | solution.py:17
  6.5 1.9 constant_dynamic-update-slice_fusion.6
  8.5 2.9 %collective-permute-done = f32[16,1,8,128]{3,2,1,0:T(8,128)S(1)} collective-permute-done((f32[16,1,8,128]{3,2,1,0:T(8,128)S(1)}, f32[16,1,8,128]{3,2,1,0:T(8,128)S(1)}, u32[]{:S(2)}, u32[]{:S(2)}) %collective-permute-start) | collective-permute-done | bytes 65568 | tf_op jit(solution)/shard_map/ppermute | solution.py:19
  13.5 4.6 %collective-permute-start.3 = (f32[16,10,1,128]{3,0,2,1:T(8,128)S(1)}, f32[16,10,1,128]{3,0,2,1:T(8,128)S(1)}, u32[]{:S(2)}, u32[]{:S(2)}) collective-permute-start(f32[16,10,1,128]{3,0,2,1:T(8,128)S(1)} %copy.268), channel_id=1, source_target_pairs={{0,8},{8,16},{16,24},{24,32},{32,40},{40,48},{48,56},{1,9},{9,17},... | collective-permute-start | bytes 245768 | tf_op jit(solution)/shard_map/ppermute | solution.py:17
  20.8 1.7 copy.231
  22.5 2.0 collective-permute-start.5
  25.3 3.6 %collective-permute-start.4 = (f32[16,10,10,1]{0,3,2,1:T(1,128)S(1)}, f32[16,10,10,1]{0,3,2,1:T(1,128)}, u32[]{:S(2)}, u32[]{:S(2)}) collective-permute-start(f32[16,10,10,1]{0,3,2,1:T(1,128)S(1)} %copy.229), channel_id=1, source_target_pairs={{1,0},{2,1},{3,2},{4,3},{5,4},{6,5},{7,6},{9,8},{10,9},{11,10},{12... | collective-permute-start | bytes 19208 | tf_op jit(solution)/shard_map/ppermute | solution.py:19
  30.7 2.0 copy.230
  32.7 3.5 %constant_dynamic-update-slice_fusion.5 = (f32[5,16,8,8,128]{4,3,2,1,0:T(8,128)}, f32[16,8,8,128]{3,2,1,0:T(8,128)S(1)}) fusion(f32[5,16,8,8,128]{4,3,2,1,0:T(8,128)} %constant_dynamic-update-slice_fusion.6, f32[16,8,8,128]{3,2,1,0:T(8,128)S(1)} %copy-done, f32[8,8,128]{2,1,0:T(8,128)S(1)} %get-tuple-element.53, f32[8,8,128]{2,1,0:T(8,128)S(1)} %get-tuple-element.54, ...), kind=kLoop, calls=%fused_computation.132 | loop fusion | flops 3932160 | bytes 2667008
  38.5 4.5 %collective-permute-start.7 = (f32[16,1,8,128]{3,2,1,0:T(8,128)S(1)}, f32[16,1,8,128]{3,2,1,0:T(8,128)S(1)}, u32[]{:S(2)}, u32[]{:S(2)}) collective-permute-start(f32[16,1,8,128]{3,2,1,0:T(8,128)S(1)} %get-tuple-element.48), channel_id=1, source_target_pairs={{0,64},{64,128},{128,192},{1,65},{65,129},{129,193},{2,66},{66,130... | collective-permute-start | bytes 196616 | tf_op jit(solution)/shard_map/ppermute | solution.py:17
  43.3 1.8 collective-permute-done.7
  46.5 4.9 %collective-permute-start.9 = (f32[16,10,1,128]{3,0,2,1:T(8,128)S(1)}, f32[16,10,1,128]{3,0,2,1:T(8,128)S(1)}, u32[]{:S(2)}, u32[]{:S(2)}) collective-permute-start(f32[16,10,1,128]{3,0,2,1:T(8,128)S(1)} %copy.235), channel_id=1, source_target_pairs={{0,8},{8,16},{16,24},{24,32},{32,40},{40,48},{48,56},{1,9},{9,17},... | collective-permute-start | bytes 245768 | tf_op jit(solution)/shard_map/ppermute | solution.py:17
  54.2 1.5 fusion.48
  55.7 2.0 copy.239
  57.7 1.9 collective-permute-start.10
  60.3 2.5 collective-permute-start.11
  64.1 1.8 collective-permute-done.11
  65.9 2.2 copy.242
  68.0 3.0 %constant_dynamic-update-slice_fusion.4 = (f32[5,16,8,8,128]{4,3,2,1,0:T(8,128)}, f32[16,8,8,128]{3,2,1,0:T(8,128)S(1)}) fusion(f32[5,16,8,8,128]{4,3,2,1,0:T(8,128)} %get-tuple-element.22, f32[16,8,8,128]{3,2,1,0:T(8,128)S(1)} %copy-done.3, f32[8,8,128]{2,1,0:T(8,128)S(1)} %get-tuple-element.53, f32[8,8,128]{2,1,0:T(8,128)S(1)} %get-tuple-element.54, ...), kind=kLoop, calls=%fused_computation.131 | loop fusion | flops 4980736 | bytes 3840256
  73.3 4.7 %collective-permute-start.13 = (f32[16,1,8,128]{3,2,1,0:T(8,128)S(1)}, f32[16,1,8,128]{3,2,1,0:T(8,128)S(1)}, u32[]{:S(2)}, u32[]{:S(2)}) collective-permute-start(f32[16,1,8,128]{3,2,1,0:T(8,128)S(1)} %get-tuple-element.46), channel_id=1, source_target_pairs={{0,64},{64,128},{128,192},{1,65},{65,129},{129,193},{2,66},{66,130... | collective-permute-start | bytes 196616 | tf_op jit(solution)/shard_map/ppermute | solution.py:17
  78.3 1.6 collective-permute-done.13
  81.4 5.0 %collective-permute-start.15 = (f32[16,10,1,128]{3,0,2,1:T(8,128)S(1)}, f32[16,10,1,128]{3,0,2,1:T(8,128)S(1)}, u32[]{:S(2)}, u32[]{:S(2)}) collective-permute-start(f32[16,10,1,128]{3,0,2,1:T(8,128)S(1)} %copy.245), channel_id=1, source_target_pairs={{0,8},{8,16},{16,24},{24,32},{32,40},{40,48},{48,56},{1,9},{9,17},... | collective-permute-start | bytes 245768 | tf_op jit(solution)/shard_map/ppermute | solution.py:17
  89.4 1.5 fusion.47
  91.0 2.0 copy.249
  92.9 2.1 collective-permute-start.16
  95.7 2.4 collective-permute-start.17
  99.4 1.8 collective-permute-done.17
  101.2 2.2 copy.252
  103.4 2.5 broadcast_multiply_fusion
  107.2 4.9 %collective-permute-start.19 = (f32[16,1,8,128]{3,2,1,0:T(8,128)S(1)}, f32[16,1,8,128]{3,2,1,0:T(8,128)S(1)}, u32[]{:S(2)}, u32[]{:S(2)}) collective-permute-start(f32[16,1,8,128]{3,2,1,0:T(8,128)S(1)} %get-tuple-element.40), channel_id=1, source_target_pairs={{0,64},{64,128},{128,192},{1,65},{65,129},{129,193},{2,66},{66,130... | collective-permute-start | bytes 196616 | tf_op jit(solution)/shard_map/ppermute | solution.py:17
  115.4 4.9 %collective-permute-start.21 = (f32[16,10,1,128]{3,0,2,1:T(8,128)S(1)}, f32[16,10,1,128]{3,0,2,1:T(8,128)S(1)}, u32[]{:S(2)}, u32[]{:S(2)}) collective-permute-start(f32[16,10,1,128]{3,0,2,1:T(8,128)S(1)} %copy.255), channel_id=1, source_target_pairs={{0,8},{8,16},{16,24},{24,32},{32,40},{40,48},{48,56},{1,9},{9,17},... | collective-permute-start | bytes 245768 | tf_op jit(solution)/shard_map/ppermute | solution.py:17
  123.3 1.5 fusion.46
  124.9 2.6 %copy.259 = f32[16,10,10,1]{0,3,2,1:T(1,128)} copy(f32[16,10,10,1]{3,2,1,0:T(8,128)} %get-tuple-element.24) | data formatting | bytes 12800 | tf_op jit(solution)/shard_map/slice | solution.py:13
  127.5 1.9 collective-permute-start.22
  130.8 2.4 collective-permute-start.23
  133.2 2.8 %pad_maximum_fusion = f32[4,16,8,8,128]{4,3,2,1,0:T(8,128)} fusion(f32[1,16,8,8,128]{4,3,2,1,0:T(8,128)} %fusion.45, f32[1,16,8,8,128]{4,3,2,1,0:T(8,128)} %get-tuple-element.44, f32[1,16,8,8,128]{4,3,2,1,0:T(8,128)S(1)} %copy-done.6, f32[1,16,8,8,128]{4,3,2,1,0:T(8,128)S(1)} %bitcast.62), kind=kLoop, calls=%fused_computation.1 | loop fusion | flops 1572864 | bytes 4194304 | tf_op jit(solution)/shard_map/stack | solution.py:69
  136.0 2.8 %slice.264 = f32[64,8192]{1,0:T(8,128)} reshape(f32[4,16,8,8,128]{4,3,2,1,0:T(8,128)} %pad_maximum_fusion) | data formatting | bytes 4194304 | tf_op jit(solution)/shard_map/slice | solution.py:74
  138.7 3.4 %copy.269 = f32[8,8,64,128]{3,2,1,0:T(8,128)} copy(f32[8,8,64,128]{3,1,2,0:T(8,128)} %bitcast.65) | data formatting | bytes 4194304
  142.1 2.0 copy.260
  144.2 3.0 %copy.262 = f32[16,10,10,1]{3,2,1,0:T(8,128)} copy(f32[16,10,10,1]{0,3,2,1:T(1,128)} %collective-permute-done.23) | data formatting | bytes 12800 | tf_op jit(solution)/shard_map/ppermute | solution.py:17
  147.2 3.0 %bitcast_dynamic-update-slice_fusion = f32[5,16,8,8,128]{4,3,2,1,0:T(8,128)} fusion(f32[5,16,8,8,128]{4,3,2,1,0:T(8,128)} %constant_dynamic-update-slice_fusion.3, f32[16,8,8,128]{3,2,1,0:T(8,128)S(1)} %get-tuple-element.19, f32[16,10,1,128]{3,2,1,0:T(1,128)S(1)} %copy-done.8, f32[16,1,8,128]{3,2,1,0:T(8,128)S(1)} %copy-done.14, ...), kind=kLoop, calls=%fused_computation.73 | loop fusion | flops 4980736 | bytes 3315968 | tf_op jit(solution)/shard_map/stack | solution.py:69
  150.2 2.6 %reshape.27 = f32[80,8192]{1,0:T(8,128)S(1)} reshape(f32[5,16,8,8,128]{4,3,2,1,0:T(8,128)} %bitcast_dynamic-update-slice_fusion) | data formatting | bytes 5242880 | tf_op jit(solution)/shard_map/reshape | solution.py:69
  152.8 2.2 fusion.55
  155.0 86.7 %psum.7 = f32[80,80]{1,0:T(8,128)S(1)} all-reduce(f32[80,80]{1,0:T(8,128)S(1)} %fusion.55), channel_id=1, replica_groups=mesh['gx'=4,'gy'=8,'gz'=8] {'gx','gy','gz'}, use_global_device_ids=true, to_apply=%region_0.0 | all-reduce | flops 6400 | bytes 51200 | tf_op jit(solution)/shard_map/psum | solution.py:72
  242.6 5.8 %cholesky.16 = f32[64,64]{1,0:T(8,128)S(1)} custom-call(f32[64,64]{1,0:T(8,128)S(1)} %fusion.13), custom_call_target="Cholesky" | custom-call | tf_op jit(solution)/shard_map/jit(cholesky)/cholesky | solution.py:42
  249.8 4.9 %custom-call.8 = f32[1,64,64]{1,2,0:T(8,128)S(1)} custom-call(f32[1,64,64]{2,1,0:T(8,128)S(1)} %fusion.8), custom_call_target="InvertDiagBlocksLowerTriangular" | custom-call | tf_op jit(solution)/shard_map/triangular_solve | solution.py:44
  255.3 1.5 fusion.2
  257.7 2.2 fusion
  (130 shorter events, 40.7 us)
Async XLA Ops:
  0.6 7.8 %copy-start = (f32[16,8,8,128]{3,2,1,0:T(8,128)S(1)}, f32[16,8,8,128]{3,2,1,0:T(8,128)}, u32[]{:S(2)}) copy-start(f32[16,8,8,128]{3,2,1,0:T(8,128)} %param.3) | copy-start | bytes 1572868
  1.6 6.8 %collective-permute-start.1 = (f32[16,1,8,128]{3,2,1,0:T(8,128)S(1)}, f32[16,1,8,128]{3,2,1,0:T(8,128)S(1)}, u32[]{:S(2)}, u32[]{:S(2)}) collective-permute-start(f32[16,1,8,128]{3,2,1,0:T(8,128)S(1)} %get-tuple-element.51), channel_id=1, source_target_pairs={{0,64},{64,128},{128,192},{1,65},{65,129},{129,193},{2,66},{66,130... | collective-permute-start | bytes 196616 | tf_op jit(solution)/shard_map/ppermute | solution.py:17
  5.1 12.9 %copy-start.20 = (f32[3,8,8,128]{3,2,1,0:T(8,128)S(1)}, f32[3,8,8,128]{3,2,1,0:T(8,128)}, u32[]{:S(2)}) copy-start(f32[3,8,8,128]{3,2,1,0:T(8,128)} %param.5) | copy-start | bytes 294916
  5.1 6.3 %collective-permute-start = (f32[16,1,8,128]{3,2,1,0:T(8,128)S(1)}, f32[16,1,8,128]{3,2,1,0:T(8,128)S(1)}, u32[]{:S(2)}, u32[]{:S(2)}) collective-permute-start(f32[16,1,8,128]{3,2,1,0:T(8,128)S(1)} %get-tuple-element.50), channel_id=1, source_target_pairs={{64,0},{128,64},{192,128},{65,1},{129,65},{193,129},{66,2},{130,66... | collective-permute-start | bytes 196616 | tf_op jit(solution)/shard_map/ppermute | solution.py:19
  11.4 0.6 copy-start.19
  12.0 8.1 %copy-start.5 = (f32[16,10,8,128]{3,2,1,0:T(8,128)}, f32[16,10,8,128]{3,2,1,0:T(8,128)S(1)}, u32[]{:S(2)}) copy-start(f32[16,10,8,128]{3,2,1,0:T(8,128)S(1)} %constant_dynamic-update-slice_fusion) | copy-start | bytes 1966084
  12.1 6.3 %collective-permute-start.2 = (f32[16,10,1,128]{3,0,2,1:T(8,128)S(1)}, f32[16,10,1,128]{3,0,2,1:T(8,128)S(1)}, u32[]{:S(2)}, u32[]{:S(2)}) collective-permute-start(f32[16,10,1,128]{3,0,2,1:T(8,128)S(1)} %copy.267), channel_id=1, source_target_pairs={{8,0},{16,8},{24,16},{32,24},{40,32},{48,40},{56,48},{9,1},{17,9},... | collective-permute-start | bytes 245768 | tf_op jit(solution)/shard_map/ppermute | solution.py:19
  13.5 6.6 %collective-permute-start.3 = (f32[16,10,1,128]{3,0,2,1:T(8,128)S(1)}, f32[16,10,1,128]{3,0,2,1:T(8,128)S(1)}, u32[]{:S(2)}, u32[]{:S(2)}) collective-permute-start(f32[16,10,1,128]{3,0,2,1:T(8,128)S(1)} %copy.268), channel_id=1, source_target_pairs={{0,8},{8,16},{16,24},{24,32},{32,40},{40,48},{48,56},{1,9},{9,17},... | collective-permute-start | bytes 245768 | tf_op jit(solution)/shard_map/ppermute | solution.py:17
  22.5 6.4 %copy-start.21 = (f32[8,8,128]{2,1,0:T(8,128)S(1)}, f32[8,8,128]{2,1,0:T(8,128)}, u32[]{:S(2)}) copy-start(f32[8,8,128]{2,1,0:T(8,128)} %param.4) | copy-start | bytes 98308
  22.5 6.4 %collective-permute-start.5 = (f32[16,10,10,1]{2,0,3,1:T(8,128)}, f32[16,10,10,1]{2,0,3,1:T(8,128)S(1)}, u32[]{:S(2)}, u32[]{:S(2)}) collective-permute-start(f32[16,10,10,1]{2,0,3,1:T(8,128)} %copy.231), channel_id=1, source_target_pairs={{0,1},{1,2},{2,3},{3,4},{4,5},{5,6},{6,7},{8,9},{9,10},{10,11},{11... | collective-permute-start | bytes 19208 | tf_op jit(solution)/shard_map/ppermute | solution.py:17
  25.3 5.4 %collective-permute-start.4 = (f32[16,10,10,1]{0,3,2,1:T(1,128)S(1)}, f32[16,10,10,1]{0,3,2,1:T(1,128)}, u32[]{:S(2)}, u32[]{:S(2)}) collective-permute-start(f32[16,10,10,1]{0,3,2,1:T(1,128)S(1)} %copy.229), channel_id=1, source_target_pairs={{1,0},{2,1},{3,2},{4,3},{5,4},{6,5},{7,6},{9,8},{10,9},{11,10},{12... | collective-permute-start | bytes 19208 | tf_op jit(solution)/shard_map/ppermute | solution.py:19
  36.2 9.0 %copy-start.2 = (f32[16,8,8,128]{3,2,1,0:T(8,128)}, f32[16,8,8,128]{3,2,1,0:T(8,128)S(1)}, u32[]{:S(2)}) copy-start(f32[16,8,8,128]{3,2,1,0:T(8,128)S(1)} %get-tuple-element.23) | copy-start | bytes 1572868
  37.2 6.2 %collective-permute-start.6 = (f32[16,1,8,128]{3,2,1,0:T(8,128)S(1)}, f32[16,1,8,128]{3,2,1,0:T(8,128)S(1)}, u32[]{:S(2)}, u32[]{:S(2)}) collective-permute-start(f32[16,1,8,128]{3,2,1,0:T(8,128)S(1)} %get-tuple-element.49), channel_id=1, source_target_pairs={{64,0},{128,64},{192,128},{65,1},{129,65},{193,129},{66,2},{130,66... | collective-permute-start | bytes 196616 | tf_op jit(solution)/shard_map/ppermute | solution.py:19
  38.5 6.6 %collective-permute-start.7 = (f32[16,1,8,128]{3,2,1,0:T(8,128)S(1)}, f32[16,1,8,128]{3,2,1,0:T(8,128)S(1)}, u32[]{:S(2)}, u32[]{:S(2)}) collective-permute-start(f32[16,1,8,128]{3,2,1,0:T(8,128)S(1)} %get-tuple-element.48), channel_id=1, source_target_pairs={{0,64},{64,128},{128,192},{1,65},{65,129},{129,193},{2,66},{66,130... | collective-permute-start | bytes 196616 | tf_op jit(solution)/shard_map/ppermute | solution.py:17
  45.2 7.4 %collective-permute-start.8 = (f32[16,10,1,128]{3,0,2,1:T(8,128)S(1)}, f32[16,10,1,128]{3,0,2,1:T(8,128)S(1)}, u32[]{:S(2)}, u32[]{:S(2)}) collective-permute-start(f32[16,10,1,128]{3,0,2,1:T(8,128)S(1)} %copy.233), channel_id=1, source_target_pairs={{8,0},{16,8},{24,16},{32,24},{40,32},{48,40},{56,48},{9,1},{17,9},... | collective-permute-start | bytes 245768 | tf_op jit(solution)/shard_map/ppermute | solution.py:19
  46.5 7.3 %collective-permute-start.9 = (f32[16,10,1,128]{3,0,2,1:T(8,128)S(1)}, f32[16,10,1,128]{3,0,2,1:T(8,128)S(1)}, u32[]{:S(2)}, u32[]{:S(2)}) collective-permute-start(f32[16,10,1,128]{3,0,2,1:T(8,128)S(1)} %copy.235), channel_id=1, source_target_pairs={{0,8},{8,16},{16,24},{24,32},{32,40},{40,48},{48,56},{1,9},{9,17},... | collective-permute-start | bytes 245768 | tf_op jit(solution)/shard_map/ppermute | solution.py:17
  57.7 5.2 %collective-permute-start.10 = (f32[16,10,10,1]{0,3,2,1:T(1,128)S(1)}, f32[16,10,10,1]{0,3,2,1:T(1,128)S(1)}, u32[]{:S(2)}, u32[]{:S(2)}) collective-permute-start(f32[16,10,10,1]{0,3,2,1:T(1,128)S(1)} %copy.239), channel_id=1, source_target_pairs={{1,0},{2,1},{3,2},{4,3},{5,4},{6,5},{7,6},{9,8},{10,9},{11,10},{12... | collective-permute-start | bytes 19208 | tf_op jit(solution)/shard_map/ppermute | solution.py:19
  60.3 7.7 %copy-start.3 = (f32[16,8,8,128]{3,2,1,0:T(8,128)S(1)}, f32[16,8,8,128]{3,2,1,0:T(8,128)}, u32[]{:S(2)}) copy-start(f32[16,8,8,128]{3,2,1,0:T(8,128)} %copy-done.2) | copy-start | bytes 1572868
  60.3 5.6 %collective-permute-start.11 = (f32[16,10,10,1]{0,3,2,1:T(1,128)S(1)}, f32[16,10,10,1]{0,3,2,1:T(1,128)S(1)}, u32[]{:S(2)}, u32[]{:S(2)}) collective-permute-start(f32[16,10,10,1]{0,3,2,1:T(1,128)S(1)} %copy.241), channel_id=1, source_target_pairs={{0,1},{1,2},{2,3},{3,4},{4,5},{5,6},{6,7},{8,9},{9,10},{10,11},{11... | collective-permute-start | bytes 19208 | tf_op jit(solution)/shard_map/ppermute | solution.py:17
  71.0 9.0 %copy-start.4 = (f32[16,8,8,128]{3,2,1,0:T(8,128)}, f32[16,8,8,128]{3,2,1,0:T(8,128)S(1)}, u32[]{:S(2)}) copy-start(f32[16,8,8,128]{3,2,1,0:T(8,128)S(1)} %get-tuple-element.21) | copy-start | bytes 1572868
  72.0 6.3 %collective-permute-start.12 = (f32[16,1,8,128]{3,2,1,0:T(8,128)S(1)}, f32[16,1,8,128]{3,2,1,0:T(8,128)S(1)}, u32[]{:S(2)}, u32[]{:S(2)}) collective-permute-start(f32[16,1,8,128]{3,2,1,0:T(8,128)S(1)} %get-tuple-element.47), channel_id=1, source_target_pairs={{64,0},{128,64},{192,128},{65,1},{129,65},{193,129},{66,2},{130,66... | collective-permute-start | bytes 196616 | tf_op jit(solution)/shard_map/ppermute | solution.py:19
  73.3 6.6 %collective-permute-start.13 = (f32[16,1,8,128]{3,2,1,0:T(8,128)S(1)}, f32[16,1,8,128]{3,2,1,0:T(8,128)S(1)}, u32[]{:S(2)}, u32[]{:S(2)}) collective-permute-start(f32[16,1,8,128]{3,2,1,0:T(8,128)S(1)} %get-tuple-element.46), channel_id=1, source_target_pairs={{0,64},{64,128},{128,192},{1,65},{65,129},{129,193},{2,66},{66,130... | collective-permute-start | bytes 196616 | tf_op jit(solution)/shard_map/ppermute | solution.py:17
  78.3 10.2 %copy-start.17 = (f32[16,1,8,128]{3,2,1,0:T(8,128)}, f32[16,1,8,128]{3,2,1,0:T(8,128)S(1)}, u32[]{:S(2)}) copy-start(f32[16,1,8,128]{3,2,1,0:T(8,128)S(1)} %collective-permute-done.12) | copy-start | bytes 196612
  79.9 8.6 %copy-start.18 = (f32[16,1,8,128]{3,2,1,0:T(8,128)}, f32[16,1,8,128]{3,2,1,0:T(8,128)S(1)}, u32[]{:S(2)}) copy-start(f32[16,1,8,128]{3,2,1,0:T(8,128)S(1)} %collective-permute-done.13) | copy-start | bytes 196612
  80.1 6.8 %collective-permute-start.14 = (f32[16,10,1,128]{3,0,2,1:T(8,128)S(1)}, f32[16,10,1,128]{3,0,2,1:T(8,128)S(1)}, u32[]{:S(2)}, u32[]{:S(2)}) collective-permute-start(f32[16,10,1,128]{3,0,2,1:T(8,128)S(1)} %copy.243), channel_id=1, source_target_pairs={{8,0},{16,8},{24,16},{32,24},{40,32},{48,40},{56,48},{9,1},{17,9},... | collective-permute-start | bytes 245768 | tf_op jit(solution)/shard_map/ppermute | solution.py:19
  81.4 7.1 %collective-permute-start.15 = (f32[16,10,1,128]{3,0,2,1:T(8,128)S(1)}, f32[16,10,1,128]{3,0,2,1:T(8,128)S(1)}, u32[]{:S(2)}, u32[]{:S(2)}) collective-permute-start(f32[16,10,1,128]{3,0,2,1:T(8,128)S(1)} %copy.245), channel_id=1, source_target_pairs={{0,8},{8,16},{16,24},{24,32},{32,40},{40,48},{48,56},{1,9},{9,17},... | collective-permute-start | bytes 245768 | tf_op jit(solution)/shard_map/ppermute | solution.py:17
  87.0 1.6 copy-start.11
  88.6 0.6 copy-start.12
  92.9 5.2 %collective-permute-start.16 = (f32[16,10,10,1]{0,3,2,1:T(1,128)S(1)}, f32[16,10,10,1]{0,3,2,1:T(1,128)S(1)}, u32[]{:S(2)}, u32[]{:S(2)}) collective-permute-start(f32[16,10,10,1]{0,3,2,1:T(1,128)S(1)} %copy.249), channel_id=1, source_target_pairs={{1,0},{2,1},{3,2},{4,3},{5,4},{6,5},{7,6},{9,8},{10,9},{11,10},{12... | collective-permute-start | bytes 19208 | tf_op jit(solution)/shard_map/ppermute | solution.py:19
  95.7 5.4 %collective-permute-start.17 = (f32[16,10,10,1]{0,3,2,1:T(1,128)S(1)}, f32[16,10,10,1]{0,3,2,1:T(1,128)S(1)}, u32[]{:S(2)}, u32[]{:S(2)}) collective-permute-start(f32[16,10,10,1]{0,3,2,1:T(1,128)S(1)} %copy.251), channel_id=1, source_target_pairs={{0,1},{1,2},{2,3},{3,4},{4,5},{5,6},{6,7},{8,9},{9,10},{10,11},{11... | collective-permute-start | bytes 19208 | tf_op jit(solution)/shard_map/ppermute | solution.py:17
  105.9 7.0 %collective-permute-start.18 = (f32[16,1,8,128]{3,2,1,0:T(8,128)S(1)}, f32[16,1,8,128]{3,2,1,0:T(8,128)S(1)}, u32[]{:S(2)}, u32[]{:S(2)}) collective-permute-start(f32[16,1,8,128]{3,2,1,0:T(8,128)S(1)} %get-tuple-element.41), channel_id=1, source_target_pairs={{64,0},{128,64},{192,128},{65,1},{129,65},{193,129},{66,2},{130,66... | collective-permute-start | bytes 196616 | tf_op jit(solution)/shard_map/ppermute | solution.py:19
  107.2 6.8 %collective-permute-start.19 = (f32[16,1,8,128]{3,2,1,0:T(8,128)S(1)}, f32[16,1,8,128]{3,2,1,0:T(8,128)S(1)}, u32[]{:S(2)}, u32[]{:S(2)}) collective-permute-start(f32[16,1,8,128]{3,2,1,0:T(8,128)S(1)} %get-tuple-element.40), channel_id=1, source_target_pairs={{0,64},{64,128},{128,192},{1,65},{65,129},{129,193},{2,66},{66,130... | collective-permute-start | bytes 196616 | tf_op jit(solution)/shard_map/ppermute | solution.py:17
  112.9 9.5 %copy-start.13 = (f32[16,1,8,128]{3,2,1,0:T(8,128)}, f32[16,1,8,128]{3,2,1,0:T(8,128)S(1)}, u32[]{:S(2)}) copy-start(f32[16,1,8,128]{3,2,1,0:T(8,128)S(1)} %collective-permute-done.18) | copy-start | bytes 196612
  114.0 8.5 %copy-start.15 = (f32[16,1,8,128]{3,2,1,0:T(8,128)}, f32[16,1,8,128]{3,2,1,0:T(8,128)S(1)}, u32[]{:S(2)}) copy-start(f32[16,1,8,128]{3,2,1,0:T(8,128)S(1)} %collective-permute-done.19) | copy-start | bytes 196612
  114.1 7.1 %collective-permute-start.20 = (f32[16,10,1,128]{3,0,2,1:T(8,128)S(1)}, f32[16,10,1,128]{3,0,2,1:T(8,128)S(1)}, u32[]{:S(2)}, u32[]{:S(2)}) collective-permute-start(f32[16,10,1,128]{3,0,2,1:T(8,128)S(1)} %copy.253), channel_id=1, source_target_pairs={{8,0},{16,8},{24,16},{32,24},{40,32},{48,40},{56,48},{9,1},{17,9},... | collective-permute-start | bytes 245768 | tf_op jit(solution)/shard_map/ppermute | solution.py:19
  115.4 7.0 %collective-permute-start.21 = (f32[16,10,1,128]{3,0,2,1:T(8,128)S(1)}, f32[16,10,1,128]{3,0,2,1:T(8,128)S(1)}, u32[]{:S(2)}, u32[]{:S(2)}) collective-permute-start(f32[16,10,1,128]{3,0,2,1:T(8,128)S(1)} %copy.255), channel_id=1, source_target_pairs={{0,8},{8,16},{16,24},{24,32},{32,40},{40,48},{48,56},{1,9},{9,17},... | collective-permute-start | bytes 245768 | tf_op jit(solution)/shard_map/ppermute | solution.py:17
  121.3 1.2 copy-start.7
  122.5 0.6 copy-start.9
  124.9 8.3 %copy-start.6 = (f32[1,16,8,8,128]{4,3,2,1,0:T(8,128)S(1)}, f32[1,16,8,8,128]{4,3,2,1,0:T(8,128)}, u32[]{:S(2)}) copy-start(f32[1,16,8,8,128]{4,3,2,1,0:T(8,128)} %get-tuple-element.42) | copy-start | bytes 1572868
  127.5 14.6 %collective-permute-start.22 = (f32[16,10,10,1]{0,3,2,1:T(1,128)}, f32[16,10,10,1]{0,3,2,1:T(1,128)}, u32[]{:S(2)}, u32[]{:S(2)}) collective-permute-start(f32[16,10,10,1]{0,3,2,1:T(1,128)} %copy.259), channel_id=1, source_target_pairs={{1,0},{2,1},{3,2},{4,3},{5,4},{6,5},{7,6},{9,8},{10,9},{11,10},{12... | collective-permute-start | bytes 19208 | tf_op jit(solution)/shard_map/ppermute | solution.py:19
  130.8 13.4 %collective-permute-start.23 = (f32[16,10,10,1]{0,3,2,1:T(1,128)}, f32[16,10,10,1]{0,3,2,1:T(1,128)}, u32[]{:S(2)}, u32[]{:S(2)}) collective-permute-start(f32[16,10,10,1]{0,3,2,1:T(1,128)} %copy.261), channel_id=1, source_target_pairs={{0,1},{1,2},{2,3},{3,4},{4,5},{5,6},{6,7},{8,9},{9,10},{10,11},{11... | collective-permute-start | bytes 19208 | tf_op jit(solution)/shard_map/ppermute | solution.py:17
  142.1 5.1 %copy-start.8 = (f32[16,10,1,128]{3,2,1,0:T(1,128)S(1)}, f32[16,10,1,128]{3,2,1,0:T(1,128)}, u32[]{:S(2)}) copy-start(f32[16,10,1,128]{3,2,1,0:T(1,128)} %copy-done.7) | copy-start | bytes 245764
  142.1 5.1 %copy-start.10 = (f32[16,10,1,128]{3,2,1,0:T(1,128)S(1)}, f32[16,10,1,128]{3,2,1,0:T(1,128)}, u32[]{:S(2)}) copy-start(f32[16,10,1,128]{3,2,1,0:T(1,128)} %copy-done.9) | copy-start | bytes 245764
  142.1 5.1 %copy-start.14 = (f32[16,1,8,128]{3,2,1,0:T(8,128)S(1)}, f32[16,1,8,128]{3,2,1,0:T(8,128)}, u32[]{:S(2)}) copy-start(f32[16,1,8,128]{3,2,1,0:T(8,128)} %copy-done.13) | copy-start | bytes 196612
  142.1 5.1 %copy-start.16 = (f32[16,1,8,128]{3,2,1,0:T(8,128)S(1)}, f32[16,1,8,128]{3,2,1,0:T(8,128)}, u32[]{:S(2)}) copy-start(f32[16,1,8,128]{3,2,1,0:T(8,128)} %copy-done.15) | copy-start | bytes 196612
  255.3 2.4 copy-start.1
where the time goes:
time: 264 us; the launch traced here: 261 us
  blocking collectives  86.7 us (33%)
  starting transfers between devices  66.4 us (25%)
  local copies, waits for them, and re-layouts  48 us (18%)
  other arithmetic  31.7 us (12%)
  waiting for transfers between devices  19.3 us (7%)
  matrix products  7.39 us (3%)
    psum x1, blocking collectives, shards(): gram = lax.psum(local_gram, ('gx', 'gy', 'gz'))  86.7 us
    ppermute x12, starting transfers between devices, extended(): lax.ppermute(tail, axis, [(i, (i + 1) % count) for i in range(ends)])  46.4 us
    ppermute x12, starting transfers between devices, extended(): lax.ppermute(head, axis, [((i + 1) % count, i) for i in range(ends)])  20 us
    slice x12, local copies, waits for them, and re-layouts, extended(): head = lax.slice_in_dim(cells, 0, width, axis=dim)  13.3 us
    ppermute x12, waiting for transfers between devices, extended(): lax.ppermute(tail, axis, [(i, (i + 1) % count) for i in range(ends)])  13.1 us
    unnamed x52, local copies, waits for them, and re-layouts  9.11 us
    ppermute x8, local copies, waits for them, and re-layouts, extended(): lax.ppermute(tail, axis, [(i, (i + 1) % count) for i in range(ends)])  8.79 us
    another operation x5, other arithmetic, shards(): basis = jnp.stack(blocks).reshape(count * (STEPS + 1), -1)  8.54 us
  transfers between devices with their start and end apart: 24, of which 16 were waited for; matrix products, arithmetic and copies ran while one was open for 8% of the time, Pallas kernels for 0%

commit v1 on v0

v1 whole, which is shorter than its diff:
```python
import jax
import jax.numpy as jnp
from jax import lax
from jax.experimental import pallas as pl
from jax.experimental.pallas import tpu as pltpu
from jax.sharding import Mesh, PartitionSpec as P

RHS = 16
STEPS = 4
COLS = RHS * (STEPS + 1)
KEEP = RHS * STEPS
FIELDS = RHS + 1
ALL = FIELDS + 5
LIMIT = 48 * 1024 * 1024
F32 = jnp.float32
BF16 = jnp.bfloat16


def lanes():
    return lax.broadcasted_iota(jnp.int32, (8, 128), 1)


def rolled(x, amount):
    amount = amount % x.shape[-1]
    return x if amount == 0 else pltpu.roll(x, amount, x.ndim - 1)


def wide(pieces):
    return jnp.concatenate(pieces, axis=0)


def pack_z(rs, ab, ve, out):
    group = lanes() // 8
    for x in range(8):
        acc = rolled(rs[x * 8 : x * 8 + 8, :], 4)
        for r in range(1, RHS):
            acc = jnp.where(group == r, rolled(rs[r * 64 + x * 8 : r * 64 + x * 8 + 8, :], 8 * r + 4), acc)
        out[x * 8 : x * 8 + 8, :] = acc
        acc = rolled(ab[x * 8 : x * 8 + 8, :], 4)
        for f in range(3):
            acc = jnp.where(
                group == f + 1, rolled(ve[f * 64 + x * 8 : f * 64 + x * 8 + 8, :], 8 * (f + 1) + 4), acc
            )
        out[64 + x * 8 : 64 + x * 8 + 8, :] = acc


def pack_xy(flags, rs, ab, ve, zprev, znext, slab, xlow, xhigh, ylow, yhigh):
    low = lanes() % 8 < 4
    zm, zp = flags[4], flags[5]
    for x in range(8):
        at = slice(x * 8, x * 8 + 8)
        slab[at, :] = jnp.where(low, zprev[at, :] * zm, znext[at, :] * zp)
        at = slice(64 + x * 8, 64 + x * 8 + 8)
        slab[at, :] = jnp.where(low, zprev[at, :], znext[at, :])

    def put(f, src, base):
        for x in range(8):
            tile = src[pl.ds(base + x * 8, 8), :]
            if x < 4:
                xlow[pl.ds(f * 32 + x * 8, 8), :] = tile
            else:
                xhigh[pl.ds(f * 32 + (x - 4) * 8, 8), :] = tile
            ylow[pl.ds(f * 32 + x * 4, 4), :] = tile[:4]
            yhigh[pl.ds(f * 32 + x * 4, 4), :] = tile[4:]

    for r in range(RHS):
        put(r, rs, r * 64)
    put(RHS, slab, 0)
    put(RHS + 1, ab, 0)
    for f in range(3):
        put(RHS + 2 + f, ve, f * 64)
    put(RHS + 5, slab, 64)


EDGES = ((-1, 3, 0), (8, 3, 3), (-2, 2, 6), (9, 2, 8), (-3, 1, 10), (10, 1, 11))


def pack_edges(xprev, xnext, ylow, yhigh):
    def body(f, carry):
        for x, rows, at in EDGES:
            src = xprev if x < 0 else xnext
            start = f * 32 + (x + 4 if x < 0 else x - 8) * 8
            tile = src[pl.ds(start, 8), :]
            ylow[pl.ds(f * 12 + at, rows), :] = tile[:rows]
            yhigh[pl.ds(f * 12 + at, rows), :] = tile[8 - rows :]
        return carry

    lax.fori_loop(0, ALL, body, 0)


def steps_gram(
    flags, rs, ab, ve, slab, xprev, xnext, yprev, ynext, eprev, enext, basis, packed, ea, eb, ec, main, side
):
    lane = lanes()
    lane8 = lane % 8
    group = lane // 8
    row = lax.broadcasted_iota(jnp.int32, (8, 128), 0)
    xm, xp, ym, yp, zm, zp = [flags[i] for i in range(6)]

    def fill(f, dst, base, src, at):
        one = jnp.float32(1)
        for x in range(8):
            dst[pl.ds(base + (x + 4) * 16 + 4, 8), :] = src[pl.ds(at + x * 8, 8), :]
            dst[pl.ds(base + (x + 4) * 16, 4), :] = yprev[pl.ds(f * 32 + x * 4, 4), :] * ym
            dst[pl.ds(base + (x + 4) * 16 + 12, 4), :] = ynext[pl.ds(f * 32 + x * 4, 4), :] * yp
        for x in range(4):
            dst[pl.ds(base + x * 16 + 4, 8), :] = xprev[pl.ds(f * 32 + x * 8, 8), :] * xm
            dst[pl.ds(base + (x + 12) * 16 + 4, 8), :] = xnext[pl.ds(f * 32 + x * 8, 8), :] * xp
        for x, rows, off in EDGES:
            m = xm if x < 0 else xp
            dst[pl.ds(base + (x + 4) * 16 + 4 - rows, rows), :] = eprev[pl.ds(f * 12 + off, rows), :] * (m * ym)
            dst[pl.ds(base + (x + 4) * 16 + 12, rows), :] = enext[pl.ds(f * 12 + off, rows), :] * (m * yp)

    def fill_rhs(r, carry):
        fill(r, ea, r * 256, rs, r * 64)
        for x in range(8):
            basis[pl.ds(x * 8 * COLS + r, 8, stride=COLS), :] = rs[pl.ds(r * 64 + x * 8, 8), :]
        return carry

    lax.fori_loop(0, RHS, fill_rhs, 0)
    fill(RHS, ea, RHS * 256, slab, 0)
    fill(RHS + 1, ec, 0, ab, 0)
    for i in range(3):
        fill(RHS + 2 + i, ec, (i + 1) * 256, ve, i * 64)
    fill(RHS + 5, ec, 4 * 256, slab, 64)

    def weights(dst, at, a, vs, ok):
        sixth = ok * F32(1 / 6)
        dst[pl.ds(at, 8), :] = (a - 1.0) * sixth
        for i in range(3):
            dst[pl.ds((2 * i + 1) * 256 + at, 8), :] = (0.5 * vs[i] - 1.0) * sixth
            dst[pl.ds((2 * i + 2) * 256 + at, 8), :] = (-0.5 * vs[i] - 1.0) * sixth

    def make(x, carry):
        okx = jnp.where(x < 4, xm, jnp.where(x >= 12, xp, F32(1)))
        for row0 in (1, 7):
            at = x * 16 + row0
            ok = okx * jnp.where(row + row0 < 4, ym, jnp.where(row + row0 >= 12, yp, F32(1)))
            vs = [ec[pl.ds((i + 1) * 256 + at, 8), :] for i in range(3)]
            weights(main, at, ec[pl.ds(at, 8), :], vs, ok)
            narrow = ec[pl.ds(4 * 256 + at, 8), :]
            spread = []
            for i in range(4):
                part = jnp.where(lane < 8, rolled(narrow, -8 * i), 0.0)
                for by in (8, 16, 32, 64):
                    part = part + rolled(part, by)
                spread.append(part)
            okz = jnp.where(lane8 < 4, zm, zp)
            weights(side, at, spread[0], spread[1:], ok * okz)
        return carry

    lax.fori_loop(1, 15, make, 0)

    for s in range(1, STEPS + 1):
        src, dst = (ea, eb) if s % 2 else (eb, ea)
        last = s == STEPS

        def plane(x, carry, s=s, src=src, dst=dst, last=last):
            for row0 in (4,) if last else (s, 8 - s):
                at = x * 16 + row0
                cm = [main[pl.ds(i * 256 + at, 8), :] for i in range(7)]
                edge = src[pl.ds(RHS * 256 + at, 8), :]

                def apply(c, base, v, zplus, zminus):
                    out = c[0] * v
                    out = out + c[1] * src[pl.ds(base + at + 16, 8), :]
                    out = out + c[2] * src[pl.ds(base + at - 16, 8), :]
                    out = out + c[3] * src[pl.ds(base + at + 1, 8), :]
                    out = out + c[4] * src[pl.ds(base + at - 1, 8), :]
                    out = out + c[5] * zplus
                    return out + c[6] * zminus

                ends = edge
                for r in range(RHS):
                    v = src[pl.ds(r * 256 + at, 8), :]
                    turn = rolled(edge, -(8 * r + 4))
                    zplus = rolled(jnp.where(lane == 0, turn, v), -1)
                    zminus = rolled(jnp.where(lane == 127, turn, v), 1)
                    out = apply(cm, r * 256, v, zplus, zminus)
                    if last:
                        first = (x - 4) * 8 * COLS + s * RHS + r
                        basis[pl.ds(first, 8, stride=COLS), :] = out
                    else:
                        dst[pl.ds(r * 256 + at, 8), :] = out
                        ends = jnp.where(group == r, rolled(v, 8 * r + 4), ends)
                if not last:
                    cs = [side[pl.ds(i * 256 + at, 8), :] for i in range(7)]
                    zplus = rolled(jnp.where(lane8 == 4, ends, edge), -1)
                    zminus = rolled(jnp.where(lane8 == 3, ends, edge), 1)
                    dst[pl.ds(RHS * 256 + at, 8), :] = apply(cs, RHS * 256, edge, zplus, zminus)
            return carry

        lax.fori_loop(s, 16 - s, plane, 0)
        if not last:

            def keep(r, carry, s=s, dst=dst):
                for x in range(8):
                    value = dst[pl.ds(r * 256 + (x + 4) * 16 + 4, 8), :]
                    basis[pl.ds(x * 8 * COLS + s * RHS + r, 8, stride=COLS), :] = value
                return carry

            lax.fori_loop(0, RHS, keep, 0)

    zeros = jnp.zeros((128 - COLS, 256), BF16)

    def product(i, acc):
        base = pl.multiple_of(i * 2 * COLS, 2 * COLS)
        value = jnp.concatenate([basis[pl.ds(base, COLS), :], basis[pl.ds(base + COLS, COLS), :]], axis=1)
        high = value.astype(BF16)
        low = (value - high.astype(F32)).astype(BF16)
        return acc + lax.dot_general(
            wide([high, low]),
            wide([high, zeros, low, zeros]),
            (((1,), (1,)), ((), ())),
            preferred_element_type=F32,
        )

    acc = lax.fori_loop(0, 32, product, jnp.zeros((2 * COLS, 256), F32))
    gram = (acc[:COLS, :128] + acc[COLS:, 128:]) + (acc[:COLS, 128:] + acc[COLS:, :128])
    part = [gram[i * RHS : (i + 1) * RHS] for i in range(STEPS + 1)]
    lane = lax.broadcasted_iota(jnp.int32, (RHS, 128), 1)
    packed[:RHS, :] = jnp.where(
        lane < 80, part[0], jnp.where(lane < 112, rolled(part[3], 32), rolled(part[4], 48))
    )
    packed[RHS:, :] = jnp.where(
        lane < 64, rolled(part[1], -16), jnp.where(lane < 112, rolled(part[2], 32), 0.0)
    )


def solve_combine(parts, basis, solution_field, residual):
    total = parts[0]
    for i in range(1, parts.shape[0]):
        total = total + parts[i]
    first, second = total[:RHS], total[RHS:]
    lane = lax.broadcasted_iota(jnp.int32, (RHS, 128), 1)

    def span(value, start):
        return jnp.where((lane >= start) & (lane < COLS), value, 0.0)

    upper = [
        span(first, 0),
        span(rolled(second, 16), 16),
        span(rolled(second, -32), 32),
        span(rolled(first, -32), 48),
        span(rolled(first, -48), 64),
    ]
    flipped = jnp.transpose(wide(upper + [jnp.zeros((128 - COLS, 128), F32)]))
    gram = wide(
        [
            jnp.where(lane < i * RHS, flipped[i * RHS : (i + 1) * RHS], upper[i])
            for i in range(STEPS + 1)
        ]
    )
    half = 7.0 * gram + 6.0 * rolled(gram, -RHS)
    half = jnp.where(lax.broadcasted_iota(jnp.int32, (COLS, 128), 1) < KEEP, half, 0.0)
    normal = 7.0 * half[:KEEP] + 6.0 * half[RHS:]
    m = [normal[i * 8 : i * 8 + 8] for i in range(8)] + [half[:8], half[8:RHS]]
    lane = lanes()
    for k in range(KEEP):
        i0, s = divmod(k, 8)
        pivot_row = m[i0][s : s + 1, :]
        inverse = 1.0 / pivot_row[:, k : k + 1]
        scaled = pivot_row * inverse
        for i in range(i0 if s < 7 else i0 + 1, 10):
            column = jnp.broadcast_to(m[i][:, k : k + 1], (8, 128))
            m[i] = jnp.where(lane == k, column * inverse, m[i] - column * scaled)
    coef = wide(m[8:])
    mixed = 7.0 * coef + 6.0 * rolled(coef, RHS)
    both = wide([coef, mixed])
    high = both.astype(BF16).astype(F32)
    low = both - high
    lane = lax.broadcasted_iota(jnp.int32, (2 * RHS, 128), 1)
    left = jnp.where(lane < 80, high, rolled(high, 80))
    right = jnp.where(lane < 32, rolled(high, -48), jnp.where(lane < 112, rolled(low, 32), 0.0))
    factors = jnp.concatenate([left, right], axis=1).astype(BF16)
    zeros = jnp.zeros((16, 256), BF16)

    def combine(i, carry):
        base = pl.multiple_of(i * 2 * COLS, 2 * COLS)
        value = jnp.concatenate([basis[pl.ds(base, COLS), :], basis[pl.ds(base + COLS, COLS), :]], axis=1)
        high = value.astype(BF16)
        low = (value - high.astype(F32)).astype(BF16)
        out = jnp.dot(factors, wide([high, low, high, zeros]), preferred_element_type=F32)
        rest = value[:RHS] - out[RHS:]
        for c in range(2):
            at = pl.ds(2 * i + c, RHS, stride=64)
            solution_field[at, :] = out[:RHS, c * 128 : (c + 1) * 128]
            residual[at, :] = rest[:, c * 128 : (c + 1) * 128]
        return carry

    lax.fori_loop(0, 32, combine, 0)


def call(kernel, ins, outs, scratch=(), smem=False):
    vmem = pl.BlockSpec(memory_space=pltpu.VMEM)
    specs = [vmem] * len(ins)
    if smem:
        specs[0] = pl.BlockSpec(memory_space=pltpu.SMEM)
    return pl.pallas_call(
        kernel,
        out_shape=[jax.ShapeDtypeStruct(s, F32) for s in outs],
        in_specs=specs,
        out_specs=[vmem] * len(outs),
        scratch_shapes=[pltpu.VMEM(s, F32) for s in scratch],
        compiler_params=pltpu.CompilerParams(vmem_limit_bytes=LIMIT),
    )(*ins)


def shift(value, axis, by):
    count = lax.axis_size(axis)
    return lax.ppermute(value, axis, [(i, (i + by) % count) for i in range(count)])


def gathered(value, axis):
    count = lax.axis_size(axis)
    return lax.all_to_all(jnp.broadcast_to(value[None], (count,) + value.shape), axis, 0, 0)


def shards(right_side, absorption, velocity):
    axes = ("gx", "gy", ("zx", "core"))
    ends = []
    for axis in axes:
        at = lax.axis_index(axis)
        ends += [at > 0, at < lax.axis_size(axis) - 1]
    flags = jnp.stack(ends).astype(F32)
    rs = right_side.reshape(1024, 128)
    ab = absorption.reshape(64, 128)
    ve = velocity.reshape(192, 128)

    (ends_z,) = call(pack_z, [rs, ab, ve], [(128, 128)])
    zprev = shift(ends_z, axes[2], 1)
    znext = shift(ends_z, axes[2], -1)
    face = (ALL * 32, 128)
    slab, xlow, xhigh, ylow, yhigh = call(
        pack_xy, [flags, rs, ab, ve, zprev, znext], [(128, 128), face, face, face, face], smem=True
    )
    xprev = shift(xhigh, "gx", 1)
    xnext = shift(xlow, "gx", -1)
    yprev = shift(yhigh, "gy", 1)
    ynext = shift(ylow, "gy", -1)
    edge = (ALL * 12, 128)
    elow, ehigh = call(pack_edges, [xprev, xnext], [edge, edge])
    eprev = shift(ehigh, "gy", 1)
    enext = shift(elow, "gy", -1)
    basis, packed = call(
        steps_gram,
        [flags, rs, ab, ve, slab, xprev, xnext, yprev, ynext, eprev, enext],
        [(64 * COLS, 128), (2 * RHS, 128)],
        [(FIELDS * 256, 128), (FIELDS * 256, 128), (5 * 256, 128), (7 * 256, 128), (7 * 256, 128)],
        smem=True,
    )
    packed = packed + shift(packed, "core", 1)
    packed = gathered(packed, ("gx", "zx")).sum(0)
    parts = gathered(packed, "gy")
    solution_field, residual = call(solve_combine, [parts, basis], [(1024, 128), (1024, 128)])
    return solution_field.reshape(right_side.shape), residual.reshape(right_side.shape)


def solution(mesh):
    nx, ny, nz = mesh.devices.shape
    split = Mesh(mesh.devices.reshape(nx, ny, nz // 2, 2), ("gx", "gy", "zx", "core"))
    z = ("zx", "core")
    return jax.shard_map(
        shards,
        mesh=split,
        in_specs=(P(None, "gx", "gy", z), P("gx", "gy", z), P(None, "gx", "gy", z)),
        out_specs=(P(None, "gx", "gy", z), P(None, "gx", "gy", z)),
        check_vma=False,
    )
```

time: 264 us -> 104 us (0.39); the launches traced: 261 us -> 104 us
  blocking collectives: 86.7 us -> 30.6 us
  starting transfers between devices: 66.4 us -> 15.1 us
  local copies, waits for them, and re-layouts: 48 us -> 5.52 us
  Pallas kernels: 0 us -> 41.1 us
  other arithmetic: 31.7 us -> 0.03 us
  waiting for transfers between devices: 19.3 us -> 10.5 us
  matrix products: 7.39 us -> 0 us
    psum x1 -> x0, blocking collectives: 86.7 us -> none  [shards(): gram = lax.psum(local_gram, ('gx', 'gy', 'gz'))]
    ppermute x24 -> x9, starting transfers between devices: 66.4 us -> 15.1 us  [shift(): lax.ppermute(value, axis, [(i, (i + by) % count) for i in range(count)])]
    pallas_call x0 -> x5, Pallas kernels: none -> 41.1 us  [call(): pl.pallas_call(kernel, out_shape=[jax.ShapeDtypeStruct(s, F32) for s in o...]
    all_to_all x0 -> x2, blocking collectives: none -> 30.6 us  [gathered(): lax.all_to_all(jnp.broadcast_to(value[None], (count,) + value.shape), axi...]
    slice x24 -> x0, local copies, waits for them, and re-layouts: 20.6 us -> none  [the longest x12 13.3 us: extended(): head = lax.slice_in_dim(cells, 0, width, axis=dim)]
    another operation x10 -> x0, other arithmetic: 20.6 us -> none  [the longest x5 8.54 us: shards(): basis = jnp.stack(blocks).reshape(count * (STEPS + 1), -1)]
    ppermute x16 -> x0, local copies, waits for them, and re-layouts: 15.6 us -> none  [the longest x8 8.79 us: extended(): lax.ppermute(tail, axis, [(i, (i + 1) % count) for i in range(ends)])]
    ppermute x24 -> x9, waiting for transfers between devices: 19.3 us -> 10.5 us  [shift(): lax.ppermute(value, axis, [(i, (i + by) % count) for i in range(count)])]
  transfers between devices with their start and end apart: 24 -> 9, of which waited for: 16 -> 5; matrix products, arithmetic and copies ran while one was open for 8% -> 0% of each run, Pallas kernels for 0% -> 0%
where the time goes in v1:
time: 104 us
  Pallas kernels  41.1 us (40%)
  blocking collectives  30.6 us (29%)
  starting transfers between devices  15.1 us (15%)
  waiting for transfers between devices  10.5 us (10%)
  local copies, waits for them, and re-layouts  5.52 us (5%)
    pallas_call x5, Pallas kernels, call(): pl.pallas_call(kernel, out_shape=[jax.ShapeDtypeStruct(s, F32) for s in o...  41.1 us
    all_to_all x2, blocking collectives, gathered(): lax.all_to_all(jnp.broadcast_to(value[None], (count,) + value.shape), axi...  30.6 us
    ppermute x9, starting transfers between devices, shift(): lax.ppermute(value, axis, [(i, (i + by) % count) for i in range(count)])  15.1 us
    ppermute x9, waiting for transfers between devices, shift(): lax.ppermute(value, axis, [(i, (i + by) % count) for i in range(count)])  10.5 us
    unnamed x14, local copies, waits for them, and re-layouts  5.38 us
  transfers between devices with their start and end apart: 9, of which 5 were waited for; matrix products, arithmetic and copies ran while one was open for 0% of the time, Pallas kernels for 0%

profile of v1, /device:TPU:2, one launch (start us, length us, event | category | flops | bytes accessed | tf_op | source)
XLA Modules:
  0.0 103.6 jit_solution(3487796961339315988)
XLA Ops:
  0.6 0.0 copy-start
  0.6 1.0 copy-done
  1.7 0.0 copy-start.3
  1.7 0.9 copy-done.3
  2.6 0.0 copy-start.5
  2.6 0.8 copy-done.5
  3.3 0.0 copy-start.2
  3.3 0.2 shard_map.50
  3.6 0.0 collective-permute-start.1
  3.6 0.5 collective-permute-start
  4.1 0.1 stack.27
  4.2 1.3 %collective-permute-done.1.znext = f32[128,128]{1,0:T(8,128)S(1)} collective-permute-done((f32[128,128]{1,0:T(8,128)S(1)}, f32[128,128]{1,0:T(8,128)S(1)}, u32[]{:S(2)}, u32[]{:S(2)}) %collective-permute-start.1) | collective-permute-done | bytes 65568 | tf_op jit(solution)/shard_map/ppermute | solution.py:311
  5.5 2.4 %collective-permute-done.zprev = f32[128,128]{1,0:T(8,128)S(1)} collective-permute-done((f32[128,128]{1,0:T(8,128)S(1)}, f32[128,128]{1,0:T(8,128)S(1)}, u32[]{:S(2)}, u32[]{:S(2)}) %collective-permute-start) | collective-permute-done | bytes 65568 | tf_op jit(solution)/shard_map/ppermute | solution.py:311
  7.9 0.0 copy-start.1
  7.9 1.0 %copy-done.1 = f32[16,8,8,128]{3,2,1,0:T(8,128)S(1)} copy-done((f32[16,8,8,128]{3,2,1,0:T(8,128)S(1)}, f32[16,8,8,128]{3,2,1,0:T(8,128)}, u32[]{:S(2)}) %copy-start.1) | copy-done | bytes 524312
  9.0 0.0 copy-start.4
  9.0 0.9 copy-done.4
  9.8 0.0 copy-start.6
  9.8 0.8 copy-done.6
  10.6 0.7 shard_map.51
  11.3 1.0 collective-permute-start.2
  12.3 2.3 %collective-permute-start.3 = (f32[704,128]{1,0:T(8,128)S(1)}, f32[704,128]{1,0:T(8,128)S(1)}, u32[]{:S(2)}, u32[]{:S(2)}) collective-permute-start(f32[704,128]{1,0:T(8,128)S(1)} %get-tuple-element.15), channel_id=1, source_target_pairs={{0,192},{64,0},{128,64},{192,128},{1,193},{65,1},{129,65},{193,129... | collective-permute-start | bytes 1081352 | tf_op jit(solution)/shard_map/ppermute | solution.py:311
  14.6 1.3 %collective-permute-start.4 = (f32[704,128]{1,0:T(8,128)S(1)}, f32[704,128]{1,0:T(8,128)S(1)}, u32[]{:S(2)}, u32[]{:S(2)}) collective-permute-start(f32[704,128]{1,0:T(8,128)S(1)} %get-tuple-element.16), channel_id=1, source_target_pairs={{0,8},{8,16},{16,24},{24,32},{32,40},{40,48},{48,56},{56,0},{1,9},... | collective-permute-start | bytes 1081352 | tf_op jit(solution)/shard_map/ppermute | solution.py:311
  15.9 3.9 %collective-permute-start.5 = (f32[704,128]{1,0:T(8,128)S(1)}, f32[704,128]{1,0:T(8,128)S(1)}, u32[]{:S(2)}, u32[]{:S(2)}) collective-permute-start(f32[704,128]{1,0:T(8,128)S(1)} %get-tuple-element.17), channel_id=1, source_target_pairs={{0,56},{8,0},{16,8},{24,16},{32,24},{40,32},{48,40},{56,48},{1,57}... | collective-permute-start | bytes 1081352 | tf_op jit(solution)/shard_map/ppermute | solution.py:311
  19.9 2.6 %collective-permute-done.2.xprev = f32[704,128]{1,0:T(8,128)S(1)} collective-permute-done((f32[704,128]{1,0:T(8,128)S(1)}, f32[704,128]{1,0:T(8,128)S(1)}, u32[]{:S(2)}, u32[]{:S(2)}) %collective-permute-start.2) | collective-permute-done | bytes 360480 | tf_op jit(solution)/shard_map/ppermute | solution.py:311
  22.5 0.0 collective-permute-done.3.xnext
  22.5 0.1 shard_map.52
  22.6 2.0 %collective-permute-start.6 = (f32[264,128]{1,0:T(8,128)S(1)}, f32[264,128]{1,0:T(8,128)S(1)}, u32[]{:S(2)}, u32[]{:S(2)}) collective-permute-start(f32[264,128]{1,0:T(8,128)S(1)} %get-tuple-element.18), channel_id=1, source_target_pairs={{0,8},{8,16},{16,24},{24,32},{32,40},{40,48},{48,56},{56,0},{1,9},... | collective-permute-start | bytes 405512 | tf_op jit(solution)/shard_map/ppermute | solution.py:311
  24.6 4.0 %collective-permute-start.7 = (f32[264,128]{1,0:T(8,128)S(1)}, f32[264,128]{1,0:T(8,128)S(1)}, u32[]{:S(2)}, u32[]{:S(2)}) collective-permute-start(f32[264,128]{1,0:T(8,128)S(1)} %get-tuple-element.19), channel_id=1, source_target_pairs={{0,56},{8,0},{16,8},{24,16},{32,24},{40,32},{48,40},{56,48},{1,57}... | collective-permute-start | bytes 405512 | tf_op jit(solution)/shard_map/ppermute | solution.py:311
  28.7 0.0 collective-permute-done.4.yprev
  28.7 0.0 collective-permute-done.5.ynext
  28.7 3.0 %collective-permute-done.6.eprev = f32[264,128]{1,0:T(8,128)S(1)} collective-permute-done((f32[264,128]{1,0:T(8,128)S(1)}, f32[264,128]{1,0:T(8,128)S(1)}, u32[]{:S(2)}, u32[]{:S(2)}) %collective-permute-start.6) | collective-permute-done | bytes 135200 | tf_op jit(solution)/shard_map/ppermute | solution.py:311
  31.7 0.0 collective-permute-done.7.enext
  31.7 0.0 copy-done.2
  31.7 24.9 %shard_map.53 = (f32[5120,128]{1,0:T(8,128)S(1)}, f32[32,128]{1,0:T(8,128)S(1)}) custom-call(f32[6]{0:T(128)S(1)} %convert_element_type.3.flags, f32[1024,128]{1,0:T(8,128)S(1)} %bitcast.13, f32[64,128]{1,0:T(8,128)S(1)} %bitcast.19, f32[192,128]{1,0:T(8,128)S(1)} %bitcast.16, f32[128,128]{1,0:T(8,128)S(1)} %get-tuple-element.13.slab, ...), custom_call_target="tpu_custom_call" | custom-call | tf_op jit(solution)/shard_map/pallas_call | solution.py:299
  56.6 0.0 collective-permute-start.8
  56.6 1.2 %collective-permute-done.8 = f32[32,128]{1,0:T(8,128)S(1)} collective-permute-done((f32[32,128]{1,0:T(8,128)S(1)}, f32[32,128]{1,0:T(8,128)S(1)}, u32[]{:S(2)}, u32[]{:S(2)}) %collective-permute-start.8) | collective-permute-done | bytes 16416 | tf_op jit(solution)/shard_map/ppermute | solution.py:311
  57.8 15.8 %all_to_all.10 = f32[16,32,128]{2,1,0:T(8,128)S(1)} all-to-all(f32[16,32,128]{2,1,0:T(8,128)S(1)} %broadcast_in_dim.4), channel_id=1, replica_groups=mesh['gx'=4,'gy'=8,'zx'=4,'core'=2] {'gx','zx'}, dimensions={0} | all-to-all | bytes 524288 | tf_op jit(solution)/shard_map/all_to_all | solution.py:316
  73.7 14.7 %all_to_all.11.parts = f32[8,32,128]{2,1,0:T(8,128)S(1)} all-to-all(f32[8,32,128]{2,1,0:T(8,128)S(1)} %broadcast_in_dim.5), channel_id=1, replica_groups=mesh['gx'=4,'gy'=8,'zx'=4,'core'=2] {'gy'}, dimensions={0} | all-to-all | bytes 262144 | tf_op jit(solution)/shard_map/all_to_all | solution.py:316
  88.4 15.2 %shard_map.54 = (f32[1024,128]{1,0:T(8,128)}, f32[1024,128]{1,0:T(8,128)}) custom-call(f32[8,32,128]{2,1,0:T(8,128)S(1)} %all_to_all.11.parts, f32[5120,128]{1,0:T(8,128)S(1)} %get-tuple-element.21.basis), custom_call_target="tpu_custom_call" | custom-call | tf_op jit(solution)/shard_map/pallas_call | solution.py:299
  (5 shorter events, 0.1 us)
Async XLA Ops:
  0.6 1.0 %copy-start = (f32[16,8,8,128]{3,2,1,0:T(8,128)S(1)}, f32[16,8,8,128]{3,2,1,0:T(8,128)}, u32[]{:S(2)}) copy-start(f32[16,8,8,128]{3,2,1,0:T(8,128)} %param.3) | copy-start | bytes 1572868
  1.7 0.9 copy-start.3
  2.6 0.8 copy-start.5
  3.3 28.3 %copy-start.2 = (f32[16,8,8,128]{3,2,1,0:T(8,128)S(1)}, f32[16,8,8,128]{3,2,1,0:T(8,128)}, u32[]{:S(2)}) copy-start(f32[16,8,8,128]{3,2,1,0:T(8,128)} %param.3) | copy-start | bytes 1572868
  3.6 1.9 %collective-permute-start.1 = (f32[128,128]{1,0:T(8,128)S(1)}, f32[128,128]{1,0:T(8,128)S(1)}, u32[]{:S(2)}, u32[]{:S(2)}) collective-permute-start(f32[128,128]{1,0:T(8,128)S(1)} %shard_map.50), channel_id=1, source_target_pairs={{0,7},{1,0},{2,1},{3,2},{4,3},{5,4},{6,5},{7,6},{8,15},{9,8},{10,9... | collective-permute-start | bytes 196616 | tf_op jit(solution)/shard_map/ppermute | solution.py:311
  3.6 4.3 %collective-permute-start = (f32[128,128]{1,0:T(8,128)S(1)}, f32[128,128]{1,0:T(8,128)S(1)}, u32[]{:S(2)}, u32[]{:S(2)}) collective-permute-start(f32[128,128]{1,0:T(8,128)S(1)} %shard_map.50), channel_id=1, source_target_pairs={{0,1},{1,2},{2,3},{3,4},{4,5},{5,6},{6,7},{7,0},{8,9},{9,10},{10,1... | collective-permute-start | bytes 196616 | tf_op jit(solution)/shard_map/ppermute | solution.py:311
  7.9 1.0 %copy-start.1 = (f32[16,8,8,128]{3,2,1,0:T(8,128)S(1)}, f32[16,8,8,128]{3,2,1,0:T(8,128)}, u32[]{:S(2)}) copy-start(f32[16,8,8,128]{3,2,1,0:T(8,128)} %param.3) | copy-start | bytes 1572868
  9.0 0.9 copy-start.4
  9.8 0.8 copy-start.6
  11.3 11.2 %collective-permute-start.2 = (f32[704,128]{1,0:T(8,128)S(1)}, f32[704,128]{1,0:T(8,128)S(1)}, u32[]{:S(2)}, u32[]{:S(2)}) collective-permute-start(f32[704,128]{1,0:T(8,128)S(1)} %get-tuple-element.14), channel_id=1, source_target_pairs={{0,64},{64,128},{128,192},{192,0},{1,65},{65,129},{129,193},{193,1... | collective-permute-start | bytes 1081352 | tf_op jit(solution)/shard_map/ppermute | solution.py:311
  12.3 10.2 %collective-permute-start.3 = (f32[704,128]{1,0:T(8,128)S(1)}, f32[704,128]{1,0:T(8,128)S(1)}, u32[]{:S(2)}, u32[]{:S(2)}) collective-permute-start(f32[704,128]{1,0:T(8,128)S(1)} %get-tuple-element.15), channel_id=1, source_target_pairs={{0,192},{64,0},{128,64},{192,128},{1,193},{65,1},{129,65},{193,129... | collective-permute-start | bytes 1081352 | tf_op jit(solution)/shard_map/ppermute | solution.py:311
  14.6 14.1 %collective-permute-start.4 = (f32[704,128]{1,0:T(8,128)S(1)}, f32[704,128]{1,0:T(8,128)S(1)}, u32[]{:S(2)}, u32[]{:S(2)}) collective-permute-start(f32[704,128]{1,0:T(8,128)S(1)} %get-tuple-element.16), channel_id=1, source_target_pairs={{0,8},{8,16},{16,24},{24,32},{32,40},{40,48},{48,56},{56,0},{1,9},... | collective-permute-start | bytes 1081352 | tf_op jit(solution)/shard_map/ppermute | solution.py:311
  15.9 12.8 %collective-permute-start.5 = (f32[704,128]{1,0:T(8,128)S(1)}, f32[704,128]{1,0:T(8,128)S(1)}, u32[]{:S(2)}, u32[]{:S(2)}) collective-permute-start(f32[704,128]{1,0:T(8,128)S(1)} %get-tuple-element.17), channel_id=1, source_target_pairs={{0,56},{8,0},{16,8},{24,16},{32,24},{40,32},{48,40},{56,48},{1,57}... | collective-permute-start | bytes 1081352 | tf_op jit(solution)/shard_map/ppermute | solution.py:311
  22.6 9.0 %collective-permute-start.6 = (f32[264,128]{1,0:T(8,128)S(1)}, f32[264,128]{1,0:T(8,128)S(1)}, u32[]{:S(2)}, u32[]{:S(2)}) collective-permute-start(f32[264,128]{1,0:T(8,128)S(1)} %get-tuple-element.18), channel_id=1, source_target_pairs={{0,8},{8,16},{16,24},{24,32},{32,40},{40,48},{48,56},{56,0},{1,9},... | collective-permute-start | bytes 405512 | tf_op jit(solution)/shard_map/ppermute | solution.py:311
  24.6 7.0 %collective-permute-start.7 = (f32[264,128]{1,0:T(8,128)S(1)}, f32[264,128]{1,0:T(8,128)S(1)}, u32[]{:S(2)}, u32[]{:S(2)}) collective-permute-start(f32[264,128]{1,0:T(8,128)S(1)} %get-tuple-element.19), channel_id=1, source_target_pairs={{0,56},{8,0},{16,8},{24,16},{32,24},{40,32},{48,40},{56,48},{1,57}... | collective-permute-start | bytes 405512 | tf_op jit(solution)/shard_map/ppermute | solution.py:311
  56.6 1.2 %collective-permute-start.8 = (f32[32,128]{1,0:T(8,128)S(1)}, f32[32,128]{1,0:T(8,128)S(1)}, u32[]{:S(2)}, u32[]{:S(2)}) collective-permute-start(f32[32,128]{1,0:T(8,128)S(1)} %get-tuple-element.20), channel_id=1, source_target_pairs={{0,1},{1,0},{2,3},{3,2},{4,5},{5,4},{6,7},{7,6},{8,9},{9,8},{10,11... | collective-permute-start | bytes 49160 | tf_op jit(solution)/shard_map/ppermute | solution.py:311
